TPU v7x, 32 devices: a whole 2x2x4 slice. The times are simulated.
32 devices in a mesh: dp: 2 (over x), expert: 4 (over y, core), mp: 4 (over z).
Axes of the slice: x: 2, y: 2, z: 4, core: 2. Of those that a mesh axis runs over, the one named last changes fastest.
Arguments:
- tokens: bfloat16 [128, 3072], P('dp'), may hold values from -6 to 6
- expert_ids: int32 [128, 2], P('dp'), may hold values from 0 to 3, all different within a row; in each aligned block of 64 rows (0 to 63, 64 to 127, ...) at most 64 rows name the same one
- gate_values: float32 [128, 2], P('dp'), may hold values from 0.2 to 1
- targets: int32 [128], P('dp'), may hold values from 0 to 32767
- w_gate: bfloat16 [4, 3072, 4, 2048], P('expert', None, 'mp', 'dp'), may hold values from -0.109375 to 0.109375
- w_up: bfloat16 [4, 3072, 4, 2048], P('expert', None, 'mp', 'dp'), may hold values from -0.109375 to 0.109375
- w_down: bfloat16 [4, 4, 2048, 3072], P('expert', 'mp', None, 'dp'), may hold values from -0.0625 to 0.0625
- norm_gain: float32 [3072], replicated, may hold values from 0.1 to 1.9
- lens_head: bfloat16 [3072, 32768], P('dp', ('expert', 'mp')), may hold values from -120 to 120
Outputs:
- mixed: bfloat16 [128, 3072], P('dp')
- log_probs: float32 [128], P('dp')
Inputs may be any that keep to these rules, and one draw needn't show every extreme that they name: `expert_ids`: each row names two different experts; in each aligned block of 64 rows no expert is named by more than 64 rows, a bound that some block reaches.
All inputs are finite; a program needn't handle non-finite values.
Results may differ from a plain program's by a relative error of at most 0.0041.
Values may be sent and summed in bfloat16 or wider, within the bound.
A program may use at most 128 MiB of HBM per device.

v0:
```python
import jax
import jax.numpy as jnp
from jax import lax
from jax.sharding import PartitionSpec as P

f32, bf16 = (jnp.float32, jnp.bfloat16)


def per_device(
    tokens, expert_ids, gate_values, targets, w_gate, w_up, w_down, norm_gain, lens_head
):
    rows, feats = tokens.shape
    owner = lax.axis_index("expert")
    weights = jnp.sum(jnp.where(expert_ids == owner, gate_values, f32(0.0)), axis=1)
    gate_mat = w_gate.reshape(feats, -1)
    up_mat = w_up.reshape(feats, -1)
    down_mat = w_down.reshape(w_down.shape[2], w_down.shape[3])
    own_feats = down_mat.shape[1]
    all_tokens = lax.all_gather(tokens, "dp", axis=0, tiled=True)
    all_weights = lax.all_gather(weights, "dp", axis=0, tiled=True)
    gate_part = jnp.dot(all_tokens, gate_mat, preferred_element_type=f32)
    up_part = jnp.dot(all_tokens, up_mat, preferred_element_type=f32)
    hidden = (jax.nn.silu(gate_part) * up_part).astype(bf16)
    hidden = lax.all_gather(hidden, "dp", axis=1, tiled=True)
    part = jnp.dot(hidden, down_mat, preferred_element_type=f32) * all_weights[:, None]
    summed = lax.psum(part, ("expert", "mp"))
    first = lax.axis_index("dp") * own_feats
    own_tokens = lax.dynamic_slice_in_dim(all_tokens, first, own_feats, axis=1)
    own_gain = lax.dynamic_slice_in_dim(norm_gain, first, own_feats, axis=0)
    mixed_part = (own_tokens.astype(f32) + summed).astype(bf16)
    mixed = lax.all_to_all(mixed_part, "dp", split_axis=0, concat_axis=1, tiled=True)
    mixed_f = mixed.astype(f32)
    scale = lax.rsqrt(jnp.mean(mixed_f * mixed_f, axis=1) + 1e-05)
    gained = (mixed_part.astype(f32) * own_gain[None, :]).astype(bf16)
    logits_part = jnp.dot(gained, lens_head, preferred_element_type=f32)
    logits = lax.psum_scatter(logits_part, "dp", scatter_dimension=0, tiled=True)
    logits = logits * scale[:, None]
    vocab_cols = lens_head.shape[1]
    vocab_start = (owner * lax.axis_size("mp") + lax.axis_index("mp")) * vocab_cols
    columns = vocab_start + lax.broadcasted_iota(jnp.int32, (1, vocab_cols), 1)
    hit = columns == targets[:, None]
    target_local = jnp.sum(jnp.where(hit, logits, f32(0.0)), axis=1)
    top = jnp.max(logits, axis=1)
    total = jnp.sum(jnp.exp(logits - top[:, None]), axis=1)
    stats = lax.all_gather(jnp.stack([top, total, target_local]), ("expert", "mp"))
    tops, totals, hits = (stats[:, 0], stats[:, 1], stats[:, 2])
    top_all = jnp.max(tops, axis=0)
    exp_total = jnp.sum(totals * jnp.exp(tops - top_all[None, :]), axis=0)
    log_probs = jnp.sum(hits, axis=0) - top_all - jnp.log(exp_total)
    return (mixed, log_probs)


def solution(mesh):
    in_specs = (
        P("dp", None),
        P("dp", None),
        P("dp", None),
        P("dp"),
        P("expert", None, "mp", "dp"),
        P("expert", None, "mp", "dp"),
        P("expert", "mp", None, "dp"),
        P(),
        P("dp", ("expert", "mp")),
    )
    out_specs = (P("dp", None), P("dp"))
    return jax.shard_map(
        per_device, mesh=mesh, in_specs=in_specs, out_specs=out_specs, check_vma=False
    )
```

profile of v0, /device:TPU:0, one launch (start us, length us, event | category | flops | bytes accessed | tf_op | source)
XLA Modules:
  0.0 207.5 jit_solution(1650163457520954662)
XLA Ops:
  7.2 0.0 all-reduce.3.cloned.1.call-start
  7.2 0.0 slice-start
  7.2 13.1 %all_gather.15 = bf16[128,3072]{1,0:T(8,128)(2,1)S(1)} all-gather(bf16[64,3072]{1,0:T(8,128)(2,1)} %param.9), channel_id=1, replica_groups=mesh['dp'=2,'expert'=4,'mp'=4] {'dp'}, dimensions={0}, use_global_device_ids=true | all-gather | bytes 1179648 | tf_op jit(solution)/shard_map/all_gather | solution.py:19
  20.3 0.0 slice-start.1
  20.3 3.9 %fusion.4 = f32[128,1024]{1,0:T(8,128)S(1)} fusion(bf16[128,3072]{1,0:T(8,128)(2,1)S(1)} %all_gather.15, bf16[1,3072,1,1024]{3,1,2,0:T(8,128)(2,1)} %param.13), kind=kOutput, calls=%fused_computation.4 | convolution fusion | flops 805306368 | bytes 7602176 | tf_op jit(solution)/shard_map/dot_general | solution.py:21
  24.2 0.0 slice-done
  24.2 0.0 slice-done.1
  24.3 0.0 copy-start.4
  24.3 0.0 copy-start.1
  24.3 0.0 copy-start.2
  24.3 1.1 fusion.12
  25.4 8.2 %all_gather.16 = bf16[128,2048]{1,0:T(8,128)(2,1)S(1)} all-gather(bf16[128,1024]{1,0:T(8,128)(2,1)S(1)} %fusion.12), channel_id=1, replica_groups=mesh['dp'=2,'expert'=4,'mp'=4] {'dp'}, dimensions={1}, use_global_device_ids=true | all-gather | bytes 786432 | tf_op jit(solution)/shard_map/all_gather | solution.py:24
  33.6 0.0 copy-done.4
  33.6 0.6 dynamic-slice
  34.8 0.0 copy-done.1
  34.8 0.0 copy-done.2
  34.9 0.2 dynamic-update-slice
  35.1 4.9 %all-reduce = f32[128]{0:T(128)S(1)} all-reduce(f32[128]{0:T(128)S(1)} %dynamic-update-slice), channel_id=1, replica_groups=mesh['dp'=2,'expert'=4,'mp'=4] {'dp'}, use_global_device_ids=true, to_apply=%add | all-reduce | flops 128 | bytes 1024
  40.0 0.0 copy-start
  40.0 4.7 %fusion.6 = f32[128,1536]{1,0:T(8,128)} fusion(bf16[128,2048]{1,0:T(8,128)(2,1)S(1)} %all_gather.16, bf16[1,1,2048,1536]{3,2,1,0:T(8,128)(2,1)} %param.15, f32[128]{0:T(128)S(1)} %all-reduce), kind=kOutput, calls=%fused_computation.6 | convolution fusion | flops 805502976 | bytes 7602688 | tf_op jit(solution)/shard_map/dot_general | solution.py:25
  44.7 0.0 all-reduce.3.cloned.1.call-update
  44.7 0.0 reduce-scatter.2.cloned.1.call-start
  44.8 0.0 copy-done
  44.8 0.1 dynamic_slice.7
  44.9 0.0 copy-start.3
  44.9 93.2 %all-reduce.3.cloned.1.call-done = f32[128,1536]{1,0:T(8,128)} async-done(((f32[128,1536]{1,0:T(8,128)}), f32[128,1536]{1,0:T(8,128)}) %all-reduce.3.cloned.1.call-update) | async-done | bytes 786448 | tf_op jit(solution)/shard_map/psum | solution.py:26
  138.1 1.9 add_convert_fusion
  140.0 4.9 %fusion.15 = f32[128,2048]{1,0:T(8,128)} fusion(bf16[1536,2048]{1,0:T(8,128)(2,1)} %param.17, bf16[128,1536]{1,0:T(8,128)(2,1)} %add_convert_fusion, f32[1536]{0:T(1024)S(1)} %dynamic_slice.7), kind=kOutput, calls=%fused_computation.15 | convolution fusion | flops 805896192 | bytes 7739392 | tf_op jit(solution)/shard_map/dot_general | solution.py:35
  144.9 0.0 reduce-scatter.2.cloned.1.call-update
  145.0 3.5 %all-to-all-start = ((bf16[2,64,1536]{2,1,0:T(8,128)(2,1)}), bf16[2,64,1536]{2,1,0:T(8,128)(2,1)S(1)}, u32[]{:S(2)}, u32[]{:S(2)}) async-start(bf16[2,64,1536]{2,1,0:T(8,128)(2,1)} %bitcast.4), calls=%async_computation | async-start | bytes 786432 | tf_op jit(solution)/shard_map/all_to_all | solution.py:31
  148.5 10.2 %all-to-all-done = bf16[2,64,1536]{2,1,0:T(8,128)(2,1)S(1)} async-done(((bf16[2,64,1536]{2,1,0:T(8,128)(2,1)}), bf16[2,64,1536]{2,1,0:T(8,128)(2,1)S(1)}, u32[]{:S(2)}, u32[]{:S(2)}) %all-to-all-start) | async-done | bytes 393248 | tf_op jit(solution)/shard_map/all_to_all | solution.py:31
  158.6 0.8 copy.16
  159.4 0.2 multiply_reduce_fusion
  159.6 7.2 %reduce-scatter.2.cloned.1.call-done = f32[64,2048]{1,0:T(8,128)} async-done(((f32[128,2048]{1,0:T(8,128)}), f32[64,2048]{1,0:T(8,128)}) %reduce-scatter.2.cloned.1.call-update) | async-done | bytes 524304 | tf_op jit(solution)/shard_map/reduce_scatter | solution.py:36
  166.8 1.2 multiply_reduce_fusion.1
  168.0 0.0 copy-done.3
  168.0 1.4 exponential_reduce_fusion
  169.4 30.6 %all-gather.1 = f32[16,3,64]{2,1,0:T(4,128)S(1)} all-gather(f32[1,3,64]{2,1,0:T(4,128)S(1)} %maximum_bitcast_fusion), channel_id=2, replica_groups=mesh['dp'=2,'expert'=4,'mp'=4] {'expert','mp'}, dimensions={0}, use_global_device_ids=true | all-gather | bytes 13056 | tf_op jit(solution)/shard_map/all_gather | solution.py:45
  200.1 0.5 log_subtract_fusion
  (8 shorter events, 0.1 us)
Async XLA Ops:
  7.2 130.9 %all-reduce.3.cloned.1.call-start = ((), (), s32[]{:S(2)}) async-start(), calls=%async_computation.2 | async-start | bytes 1572864 | tf_op jit(solution)/shard_map/psum | solution.py:26
  7.2 17.0 %slice-start = ((s8[6291456]{0:T(1024)(128)(4,1)}), s8[4194304]{0:T(1024)(128)(4,1)S(1)}, s32[]{:S(2)}) async-start(s8[6291456]{0:T(1024)(128)(4,1)} %bitcast.41), calls=%async_computation.4 | async-start | bytes 8388608
  20.3 3.9 %slice-start.1 = ((s8[6291456]{0:T(1024)(128)(4,1)}), s8[2097152]{0:T(1024)(128)(4,1)S(1)}, s32[]{:S(2)}) async-start(s8[6291456]{0:T(1024)(128)(4,1)} %bitcast.41), calls=%async_computation.5 | async-start | bytes 4194304
  24.3 9.3 %copy-start.4 = (u32[32]{0:T(128)S(1)}, u32[32]{0:T(128)}, u32[]{:S(2)}) copy-start(u32[32]{0:T(128)} %constant.40) | copy-start | bytes 388
  24.3 10.5 %copy-start.1 = (f32[64,2]{0,1:T(2,128)S(1)}, f32[64,2]{0,1:T(2,128)}, u32[]{:S(2)}) copy-start(f32[64,2]{0,1:T(2,128)} %param.11) | copy-start | bytes 1540
  24.3 10.5 %copy-start.2 = (s32[64,2]{0,1:T(2,128)S(1)}, s32[64,2]{0,1:T(2,128)}, u32[]{:S(2)}) copy-start(s32[64,2]{0,1:T(2,128)} %param.10) | copy-start | bytes 1540
  40.0 4.8 %copy-start = (f32[3072]{0:T(1024)S(1)}, f32[3072]{0:T(1024)}, u32[]{:S(2)}) copy-start(f32[3072]{0:T(1024)} %param.16) | copy-start | bytes 36868
  44.7 122.0 %reduce-scatter.2.cloned.1.call-start = ((), (), s32[]{:S(2)}) async-start(), calls=%async_computation.3 | async-start | bytes 1572864 | tf_op jit(solution)/shard_map/reduce_scatter | solution.py:36
  44.9 123.1 %copy-start.3 = (s32[64]{0:T(128)S(1)}, s32[64]{0:T(128)}, u32[]{:S(2)}) copy-start(s32[64]{0:T(128)} %param.12) | copy-start | bytes 772
  145.0 13.7 %all-to-all-start = ((bf16[2,64,1536]{2,1,0:T(8,128)(2,1)}), bf16[2,64,1536]{2,1,0:T(8,128)(2,1)S(1)}, u32[]{:S(2)}, u32[]{:S(2)}) async-start(bf16[2,64,1536]{2,1,0:T(8,128)(2,1)} %bitcast.4), calls=%async_computation | async-start | bytes 786432 | tf_op jit(solution)/shard_map/all_to_all | solution.py:31
Sparse Core Ops, SparseCore 0:
  44.9 93.1 all-reduce.2
  145.1 21.6 reduce-scatter.1
where the time goes:
time: 208 us; the launch traced here: 207 us
  waiting for transfers between devices  111 us (53%)
  blocking collectives  56.8 us (27%)
  between operations  14.9 us (7%)
  matrix products  14.6 us (7%)
  other arithmetic  5.39 us (3%)
  starting transfers between devices  3.56 us (2%)
    psum x1, waiting for transfers between devices, per_device(): summed = lax.psum(part, ('expert', 'mp'))  93.2 us
    all_gather x1, blocking collectives, per_device(): lax.all_gather(jnp.stack([top, total, target_local]), ('expert', 'mp'))  30.6 us
    all_gather x1, blocking collectives, per_device(): all_tokens = lax.all_gather(tokens, 'dp', axis=0, tiled=True)  13.1 us
    all_to_all x1, waiting for transfers between devices, per_device(): lax.all_to_all(mixed_part, 'dp', split_axis=0, concat_axis=1, tiled=True)  10.2 us
    all_gather x1, blocking collectives, per_device(): hidden = lax.all_gather(hidden, 'dp', axis=1, tiled=True)  8.17 us
    reduce_scatter x1, waiting for transfers between devices, per_device(): lax.psum_scatter(logits_part, 'dp', scatter_dimension=0, tiled=True)  7.19 us
    unnamed x1, blocking collectives  4.92 us
    dot_general x1, matrix products, per_device(): logits_part = jnp.dot(gained, lens_head, preferred_element_type=f32)  4.91 us
  transfers between devices with their start and end apart: 3, of which 3 were waited for; matrix products, arithmetic and copies ran while one was open for 1% of the time, Pallas kernels for 0%

commit v1 on v0

--- a/solution.py
+++ b/solution.py
@@ -23,7 +23,7 @@
     hidden = (jax.nn.silu(gate_part) * up_part).astype(bf16)
     hidden = lax.all_gather(hidden, "dp", axis=1, tiled=True)
     part = jnp.dot(hidden, down_mat, preferred_element_type=f32) * all_weights[:, None]
-    summed = lax.psum(part, ("expert", "mp"))
+    summed = lax.psum(lax.psum(part, "mp"), "expert")
     first = lax.axis_index("dp") * own_feats
     own_tokens = lax.dynamic_slice_in_dim(all_tokens, first, own_feats, axis=1)
     own_gain = lax.dynamic_slice_in_dim(norm_gain, first, own_feats, axis=0)

time: 208 us -> 197 us (0.947)
  waiting for transfers between devices: 111 us -> 98.4 us
    psum x1 -> x2, waiting for transfers between devices: 93.2 us -> 81.2 us  [per_device(): summed = lax.psum(lax.psum(part, 'mp'), 'expert')]
  transfers between devices with their start and end apart: 3 -> 4, of which waited for: 3 -> 4; matrix products, arithmetic and copies ran while one was open for 1% -> 1% of each run, Pallas kernels for 0% -> 0%
where the time goes in v1:
time: 197 us
  waiting for transfers between devices  98.4 us (50%)
  blocking collectives  58.4 us (30%)
  matrix products  14.6 us (7%)
  between operations  14.6 us (7%)
  other arithmetic  5.39 us (3%)
  starting transfers between devices  3.6 us (2%)
    psum x2, waiting for transfers between devices, per_device(): summed = lax.psum(lax.psum(part, 'mp'), 'expert')  81.2 us
    all_gather x1, blocking collectives, per_device(): lax.all_gather(jnp.stack([top, total, target_local]), ('expert', 'mp'))  32.2 us
    all_gather x1, blocking collectives, per_device(): all_tokens = lax.all_gather(tokens, 'dp', axis=0, tiled=True)  13.1 us
    reduce_scatter x1, waiting for transfers between devices, per_device(): lax.psum_scatter(logits_part, 'dp', scatter_dimension=0, tiled=True)  9.06 us
    all_to_all x1, waiting for transfers between devices, per_device(): lax.all_to_all(mixed_part, 'dp', split_axis=0, concat_axis=1, tiled=True)  8.18 us
    all_gather x1, blocking collectives, per_device(): hidden = lax.all_gather(hidden, 'dp', axis=1, tiled=True)  8.17 us
    unnamed x1, blocking collectives  4.92 us
    dot_general x1, matrix products, per_device(): logits_part = jnp.dot(gained, lens_head, preferred_element_type=f32)  4.91 us
  transfers between devices with their start and end apart: 4, of which 4 were waited for; matrix products, arithmetic and copies ran while one was open for 1% of the time, Pallas kernels for 0%

profile of v1, /device:TPU:0, one launch (start us, length us, event | category | flops | bytes accessed | tf_op | source)
XLA Modules:
  0.0 196.7 jit_solution(14776009412464102762)
XLA Ops:
  7.2 0.0 all-reduce.4.cloned.1.call-start
  7.2 0.0 slice-start
  7.2 13.1 %all_gather.15 = bf16[128,3072]{1,0:T(8,128)(2,1)S(1)} all-gather(bf16[64,3072]{1,0:T(8,128)(2,1)} %param.9), channel_id=1, replica_groups=mesh['dp'=2,'expert'=4,'mp'=4] {'dp'}, dimensions={0}, use_global_device_ids=true | all-gather | bytes 1179648 | tf_op jit(solution)/shard_map/all_gather | solution.py:19
  20.3 0.0 slice-start.1
  20.3 3.9 %fusion.4 = f32[128,1024]{1,0:T(8,128)S(1)} fusion(bf16[128,3072]{1,0:T(8,128)(2,1)S(1)} %all_gather.15, bf16[1,3072,1,1024]{3,1,2,0:T(8,128)(2,1)} %param.13), kind=kOutput, calls=%fused_computation.4 | convolution fusion | flops 805306368 | bytes 7602176 | tf_op jit(solution)/shard_map/dot_general | solution.py:21
  24.2 0.0 slice-done
  24.2 0.0 slice-done.1
  24.3 0.0 copy-start.4
  24.3 0.0 copy-start.1
  24.3 0.0 copy-start.2
  24.3 1.1 fusion.12
  25.4 8.2 %all_gather.16 = bf16[128,2048]{1,0:T(8,128)(2,1)S(1)} all-gather(bf16[128,1024]{1,0:T(8,128)(2,1)S(1)} %fusion.12), channel_id=1, replica_groups=mesh['dp'=2,'expert'=4,'mp'=4] {'dp'}, dimensions={1}, use_global_device_ids=true | all-gather | bytes 786432 | tf_op jit(solution)/shard_map/all_gather | solution.py:24
  33.6 0.0 copy-done.4
  33.6 0.6 dynamic-slice
  34.8 0.0 copy-done.1
  34.8 0.0 copy-done.2
  34.9 0.2 dynamic-update-slice
  35.1 4.9 %all-reduce = f32[128]{0:T(128)S(1)} all-reduce(f32[128]{0:T(128)S(1)} %dynamic-update-slice), channel_id=1, replica_groups=mesh['dp'=2,'expert'=4,'mp'=4] {'dp'}, use_global_device_ids=true, to_apply=%add | all-reduce | flops 128 | bytes 1024
  40.0 0.0 copy-start
  40.0 4.7 %fusion.6 = f32[128,1536]{1,0:T(8,128)} fusion(bf16[128,2048]{1,0:T(8,128)(2,1)S(1)} %all_gather.16, bf16[1,1,2048,1536]{3,2,1,0:T(8,128)(2,1)} %param.15, f32[128]{0:T(128)S(1)} %all-reduce), kind=kOutput, calls=%fused_computation.6 | convolution fusion | flops 805502976 | bytes 7602688 | tf_op jit(solution)/shard_map/dot_general | solution.py:25
  44.7 0.0 all-reduce.4.cloned.1.call-update
  44.7 0.0 all-reduce.6.cloned.1.call-start
  44.8 45.0 %all-reduce.4.cloned.1.call-done = f32[128,1536]{1,0:T(8,128)} async-done(((f32[128,1536]{1,0:T(8,128)}), f32[128,1536]{1,0:T(8,128)}) %all-reduce.4.cloned.1.call-update) | async-done | bytes 786448 | tf_op jit(solution)/shard_map/psum | solution.py:26
  89.7 0.0 all-reduce.6.cloned.1.call-update
  89.8 0.0 reduce-scatter.2.cloned.1.call-start
  89.8 0.0 copy-done
  89.8 0.1 dynamic_slice.7
  89.9 0.0 copy-start.3
  89.9 36.2 %all-reduce.6.cloned.1.call-done = f32[128,1536]{1,0:T(8,128)} async-done(((f32[128,1536]{1,0:T(8,128)}), f32[128,1536]{1,0:T(8,128)}) %all-reduce.6.cloned.1.call-update) | async-done | bytes 786448 | tf_op jit(solution)/shard_map/psum | solution.py:26
  126.1 1.9 add_convert_fusion
  128.1 4.9 %fusion.15 = f32[128,2048]{1,0:T(8,128)} fusion(bf16[1536,2048]{1,0:T(8,128)(2,1)} %param.17, bf16[128,1536]{1,0:T(8,128)(2,1)} %add_convert_fusion, f32[1536]{0:T(1024)S(1)} %dynamic_slice.7), kind=kOutput, calls=%fused_computation.15 | convolution fusion | flops 805896192 | bytes 7739392 | tf_op jit(solution)/shard_map/dot_general | solution.py:35
  133.0 0.0 reduce-scatter.2.cloned.1.call-update
  133.0 3.5 %all-to-all-start = ((bf16[2,64,1536]{2,1,0:T(8,128)(2,1)}), bf16[2,64,1536]{2,1,0:T(8,128)(2,1)S(1)}, u32[]{:S(2)}, u32[]{:S(2)}) async-start(bf16[2,64,1536]{2,1,0:T(8,128)(2,1)} %bitcast.4), calls=%async_computation | async-start | bytes 786432 | tf_op jit(solution)/shard_map/all_to_all | solution.py:31
  136.5 8.2 %all-to-all-done = bf16[2,64,1536]{2,1,0:T(8,128)(2,1)S(1)} async-done(((bf16[2,64,1536]{2,1,0:T(8,128)(2,1)}), bf16[2,64,1536]{2,1,0:T(8,128)(2,1)S(1)}, u32[]{:S(2)}, u32[]{:S(2)}) %all-to-all-start) | async-done | bytes 393248 | tf_op jit(solution)/shard_map/all_to_all | solution.py:31
  144.7 0.8 copy.16
  145.5 0.2 multiply_reduce_fusion
  145.6 9.1 %reduce-scatter.2.cloned.1.call-done = f32[64,2048]{1,0:T(8,128)} async-done(((f32[128,2048]{1,0:T(8,128)}), f32[64,2048]{1,0:T(8,128)}) %reduce-scatter.2.cloned.1.call-update) | async-done | bytes 524304 | tf_op jit(solution)/shard_map/reduce_scatter | solution.py:36
  154.7 1.2 multiply_reduce_fusion.1
  156.0 0.0 copy-done.3
  156.0 1.4 exponential_reduce_fusion
  157.4 32.2 %all-gather.1 = f32[16,3,64]{2,1,0:T(4,128)S(1)} all-gather(f32[1,3,64]{2,1,0:T(4,128)S(1)} %maximum_bitcast_fusion), channel_id=2, replica_groups=mesh['dp'=2,'expert'=4,'mp'=4] {'expert','mp'}, dimensions={0}, use_global_device_ids=true | all-gather | bytes 13056 | tf_op jit(solution)/shard_map/all_gather | solution.py:45
  189.6 0.5 log_subtract_fusion
  (8 shorter events, 0.1 us)
Async XLA Ops:
  7.2 82.6 %all-reduce.4.cloned.1.call-start = ((), (), s32[]{:S(2)}) async-start(), calls=%async_computation.2 | async-start | bytes 1572864 | tf_op jit(solution)/shard_map/psum | solution.py:26
  7.2 17.0 %slice-start = ((s8[6291456]{0:T(1024)(128)(4,1)}), s8[4194304]{0:T(1024)(128)(4,1)S(1)}, s32[]{:S(2)}) async-start(s8[6291456]{0:T(1024)(128)(4,1)} %bitcast.41), calls=%async_computation.5 | async-start | bytes 8388608
  20.3 3.9 %slice-start.1 = ((s8[6291456]{0:T(1024)(128)(4,1)}), s8[2097152]{0:T(1024)(128)(4,1)S(1)}, s32[]{:S(2)}) async-start(s8[6291456]{0:T(1024)(128)(4,1)} %bitcast.41), calls=%async_computation.6 | async-start | bytes 4194304
  24.3 9.3 %copy-start.4 = (u32[32]{0:T(128)S(1)}, u32[32]{0:T(128)}, u32[]{:S(2)}) copy-start(u32[32]{0:T(128)} %constant.40) | copy-start | bytes 388
  24.3 10.5 %copy-start.1 = (f32[64,2]{0,1:T(2,128)S(1)}, f32[64,2]{0,1:T(2,128)}, u32[]{:S(2)}) copy-start(f32[64,2]{0,1:T(2,128)} %param.11) | copy-start | bytes 1540
  24.3 10.5 %copy-start.2 = (s32[64,2]{0,1:T(2,128)S(1)}, s32[64,2]{0,1:T(2,128)}, u32[]{:S(2)}) copy-start(s32[64,2]{0,1:T(2,128)} %param.10) | copy-start | bytes 1540
  40.0 49.8 %copy-start = (f32[3072]{0:T(1024)S(1)}, f32[3072]{0:T(1024)}, u32[]{:S(2)}) copy-start(f32[3072]{0:T(1024)} %param.16) | copy-start | bytes 36868
  44.7 81.4 %all-reduce.6.cloned.1.call-start = ((), (), s32[]{:S(2)}) async-start(), calls=%async_computation.3 | async-start | bytes 1572864 | tf_op jit(solution)/shard_map/psum | solution.py:26
  89.8 64.9 %reduce-scatter.2.cloned.1.call-start = ((), (), s32[]{:S(2)}) async-start(), calls=%async_computation.4 | async-start | bytes 1572864 | tf_op jit(solution)/shard_map/reduce_scatter | solution.py:36
  89.9 66.0 %copy-start.3 = (s32[64]{0:T(128)S(1)}, s32[64]{0:T(128)}, u32[]{:S(2)}) copy-start(s32[64]{0:T(128)} %param.12) | copy-start | bytes 772
  133.0 11.7 %all-to-all-start = ((bf16[2,64,1536]{2,1,0:T(8,128)(2,1)}), bf16[2,64,1536]{2,1,0:T(8,128)(2,1)S(1)}, u32[]{:S(2)}, u32[]{:S(2)}) async-start(bf16[2,64,1536]{2,1,0:T(8,128)(2,1)} %bitcast.4), calls=%async_computation | async-start | bytes 786432 | tf_op jit(solution)/shard_map/all_to_all | solution.py:31
Sparse Core Ops, SparseCore 0:
  44.9 44.8 all-reduce.3
  92.1 33.9 all-reduce.5
  133.1 21.5 reduce-scatter.1
